TPU v7x, 32 devices: a whole 2x2x4 slice. The times are simulated.
32 devices in a mesh: dp: 2 (over y), place: 16 (over z, x, core).
Axes of the slice: x: 2, y: 2, z: 4, core: 2. Of those that a mesh axis runs over, the one named last changes fastest.
Arguments:
- tokens: bfloat16 [2, 16, 256, 2048], P('dp', 'place'), may hold values from -6 to 6
- hidden_grad: bfloat16 [2, 16, 256, 256], P('dp', 'place'), may hold values from -6 to 6
- routing: int32 [2, 16, 4, 64], P('dp', 'place'), may hold values from 0 to 63, each once within a row
- row_count: int32 [2, 16], replicated, may hold values from 1 to 256, as said below
- old_slots: int32 [16], replicated, may hold values from 0 to 3, as said below
- new_slots: int32 [16], replicated, may hold values from 0 to 3, as said below
- master: float32 [4, 2048, 512], P(None, ('dp', 'place')), may hold values from -0.125 to 0.125
- first_moment: float32 [4, 2048, 512], P(None, ('dp', 'place')), may hold values from -0.018 to 0.018
- second_moment: float32 [4, 2048, 512], P(None, ('dp', 'place')), may hold values from 1e-06 to 0.0001
Outputs:
- new_weights: bfloat16 [16, 2048, 512], P('place')
- new_master: float32 [4, 2048, 512], P(None, ('dp', 'place'))
- new_first: float32 [4, 2048, 512], P(None, ('dp', 'place'))
- new_second: float32 [4, 2048, 512], P(None, ('dp', 'place'))
Inputs may be any that keep to these rules, and one draw needn't show every extreme that they name: `old_slots`: every expert 0 .. 3 holds at least one slot. `new_slots`: every expert 0 .. 3 holds at least one slot. The first row_count[d, p] of a device's 256 row slots are live; some device is full in every draw.
All inputs are finite; a program needn't handle non-finite values.
Results may differ from a plain program's by a relative error of at most 0.001.
The roundings to bfloat16 on the way count: a program that leaves them out, or rounds other values in their place, can miss the bound.
Values may be sent and summed in bfloat16 or wider, within the bound.
A program may use at most 64 MiB of HBM per device.

v0:
```python
import jax
import jax.numpy as jnp
from jax import lax
from jax.sharding import PartitionSpec as P

decay_first = 0.9
decay_second = 0.95
learn_rate = 0.001
weight_decay = 0.1
epsilon = 1e-08
step_number = 20.0


def spread(shard, slots):
    experts, rows_shard, width = shard.shape
    places = lax.axis_size("place")
    select = (slots[:, None] == jnp.arange(experts, dtype=jnp.int32)[None, :]).astype(jnp.bfloat16)
    picked = jnp.dot(
        select, shard.reshape(experts, rows_shard * width), preferred_element_type=jnp.float32
    ).astype(jnp.bfloat16)
    landed = lax.all_to_all(
        picked.reshape(places, rows_shard, width), "place", split_axis=0, concat_axis=0, tiled=True
    )
    whole = lax.all_gather(landed.reshape(places * rows_shard, width), "dp", axis=0, tiled=True)
    return whole


def batch_grad(total, rows_in, grads_in, order, count, weights, start):
    rows = order.shape[0]
    half = weights.shape[1] // 2
    picked = jnp.take(rows_in, start + order, axis=0)
    both = jnp.dot(picked, weights, preferred_element_type=jnp.float32)
    gate = both[:, :half]
    upward = both[:, half:]
    sigma = jax.nn.sigmoid(gate)
    active = gate * sigma
    slope = sigma * (1.0 + gate * (1.0 - sigma))
    live = start + jnp.arange(rows, dtype=jnp.int32) < count
    incoming = jnp.where(live[:, None], grads_in[start : start + rows].astype(jnp.float32), 0.0)
    local = jnp.concatenate([incoming * upward * slope, incoming * active], axis=1).astype(
        jnp.bfloat16
    )
    return total + lax.dot_general(
        picked, local, (((0,), (0,)), ((), ())), preferred_element_type=jnp.float32
    )


def shards(
    tokens,
    hidden_grad,
    routing,
    row_count,
    old_slots,
    new_slots,
    master,
    first_moment,
    second_moment,
):
    places = lax.axis_size("place")
    groups = lax.axis_size("dp")
    experts, rows_shard, width = master.shape
    place_here = lax.axis_index("place")
    group_here = lax.axis_index("dp")
    weights = spread(master.astype(jnp.bfloat16), old_slots)
    rows_in = tokens[0, 0]
    grads_in = hidden_grad[0, 0]
    order = routing[0, 0]
    count = row_count[group_here, place_here]
    batch_rows = order.shape[1]
    summed = jnp.zeros((rows_in.shape[1], width), jnp.float32)
    for batch_index in range(order.shape[0]):
        start = batch_index * batch_rows
        summed = batch_grad(summed, rows_in, grads_in, order[batch_index], count, weights, start)
    select = (old_slots[:, None] == jnp.arange(experts, dtype=jnp.int32)[None, :]).astype(
        jnp.float32
    )
    blocks = summed.reshape(groups, places, rows_shard, width)
    landed = lax.all_to_all(blocks, "place", split_axis=1, concat_axis=1, tiled=True)
    merged = jnp.einsum(
        "se,dsx->dex",
        select,
        landed.reshape(groups, places, rows_shard * width),
        precision=lax.Precision.HIGHEST,
    )
    mine = lax.psum_scatter(merged, "dp", scatter_dimension=0, tiled=True)
    grad_sum = mine.reshape(experts, rows_shard, width)
    per_slot = jnp.sum(row_count.astype(jnp.float32), axis=0)
    total = jnp.dot(per_slot, select, precision=lax.Precision.HIGHEST)
    grad = grad_sum / total[:, None, None]
    new_first = decay_first * first_moment + (1.0 - decay_first) * grad
    new_second = decay_second * second_moment + (1.0 - decay_second) * grad * grad
    first_hat = new_first / (1.0 - decay_first**step_number)
    second_hat = new_second / (1.0 - decay_second**step_number)
    new_master = master - learn_rate * (
        first_hat / (jnp.sqrt(second_hat) + epsilon) + weight_decay * master
    )
    new_weights = spread(new_master.astype(jnp.bfloat16), new_slots)
    return (new_weights[None], new_master, new_first, new_second)


def solution(mesh):
    placed = (
        P("dp", "place", None, None),
        P("dp", "place", None, None),
        P("dp", "place", None, None),
        P(),
        P(),
        P(),
        P(None, ("dp", "place"), None),
        P(None, ("dp", "place"), None),
        P(None, ("dp", "place"), None),
    )
    return jax.shard_map(
        shards,
        mesh=mesh,
        in_specs=placed,
        out_specs=(
            P("place", None, None),
            P(None, ("dp", "place"), None),
            P(None, ("dp", "place"), None),
            P(None, ("dp", "place"), None),
        ),
        check_vma=False,
    )
```

profile of v0, /device:TPU:1, one launch (start us, length us, event | category | flops | bytes accessed | tf_op | source)
XLA Modules:
  0.0 313.2 jit_solution(2663742370187234201)
XLA Ops:
  7.2 0.0 copy-start
  7.2 0.0 all-gather.3.cloned.1.call-start
  7.2 1.2 convert_bitcast_fusion.1
  8.4 0.2 copy.16
  8.6 1.2 convolution_convert_fusion.1
  9.8 0.3 copy.17
  10.1 32.4 %all_to_all.15 = bf16[16,64,512]{2,1,0:T(8,128)(2,1)} all-to-all(bf16[16,64,512]{2,1,0:T(8,128)(2,1)S(1)} %bitcast.83), channel_id=1, replica_groups=mesh['dp'=2,'place'=16] {'place'}, dimensions={0} | all-to-all | bytes 2097152 | tf_op jit(solution)/shard_map/all_to_all | solution.py:21
  42.5 0.0 all-gather.3.cloned.1.call-update
  42.6 0.0 all-reduce.3.cloned.1.call-start
  42.7 0.0 copy-start.9
  42.7 0.7 gather_fusion
  43.4 0.7 gather_fusion.1
  44.2 0.7 gather_fusion.3
  44.9 0.7 gather_fusion.2
  45.7 0.0 copy-start.5
  45.7 0.6 dynamic_slice.3
  46.3 0.7 add_compare_fusion
  47.0 0.7 add_compare_fusion.2
  47.6 27.6 %all-gather.3.cloned.1.call-done = bf16[2048,512]{1,0:T(8,128)(2,1)} async-done(((bf16[1024,512]{1,0:T(8,128)(2,1)}), bf16[2048,512]{1,0:T(8,128)(2,1)}) %all-gather.3.cloned.1.call-update) | async-done | bytes 2097168 | tf_op jit(solution)/shard_map/all_gather | solution.py:24
  75.2 2.3 fusion.3
  77.5 2.1 fusion.5
  79.6 0.5 fusion.8
  80.2 0.1 fusion.10
  80.3 0.8 fusion.4
  81.1 0.8 fusion.2
  82.0 0.5 fusion.7
  82.5 0.1 fusion.12
  82.6 0.8 fusion.6
  83.4 0.8 add_add_fusion
  84.2 0.6 copy.13
  84.8 98.7 %all_to_all.16 = f32[2,16,64,512]{3,2,0,1:T(8,128)} all-to-all(f32[2,16,64,512]{3,2,0,1:T(8,128)S(1)} %copy.13), channel_id=1, replica_groups=mesh['dp'=2,'place'=16] {'place'}, dimensions={1} | all-to-all | bytes 8388608 | tf_op jit(solution)/shard_map/all_to_all | solution.py:78
  183.5 6.7 %reshape.148 = f32[2,16,32768]{2,0,1:T(2,128)} reshape(f32[2,16,64,512]{3,2,0,1:T(8,128)} %all_to_all.16) | data formatting | bytes 8388608 | tf_op jit(solution)/shard_map/reshape | solution.py:82
  190.2 0.0 copy-start.4
  190.2 6.9 %convolution_bitcast_fusion = f32[2,4,32768]{2,1,0:T(4,128)} fusion(f32[2,16,32768]{2,0,1:T(2,128)} %reshape.148, s32[16]{0:T(128)S(1)} %copy-done.7), kind=kOutput, calls=%fused_computation.6 | convolution fusion | flops 50331712 | bytes 5242944 | tf_op jit(solution)/shard_map/se,dsx->dex/dot_general | solution.py:79
  197.1 0.0 all-reduce.3.cloned.1.call-update
  197.2 0.0 all-gather.5.cloned.1.call-start
  197.2 0.6 dynamic-slice
  197.8 0.1 convolution_bitcast_fusion.1
  197.9 38.2 %all-reduce.3.cloned.1.call-done = f32[2,4,32768]{2,1,0:T(4,128)} async-done(((f32[2,4,32768]{2,1,0:T(4,128)}), f32[2,4,32768]{2,1,0:T(4,128)}) %all-reduce.3.cloned.1.call-update) | async-done | bytes 1048592
  236.1 1.7 constant_dynamic-slice_fusion
  237.9 1.6 convert_bitcast_fusion
  239.5 0.2 copy.19
  239.7 0.5 convolution_convert_fusion
  240.2 0.3 copy.20
  240.5 31.3 %all_to_all.17 = bf16[16,64,512]{2,1,0:T(8,128)(2,1)} all-to-all(bf16[16,64,512]{2,1,0:T(8,128)(2,1)S(1)} %bitcast.85), channel_id=1, replica_groups=mesh['dp'=2,'place'=16] {'place'}, dimensions={0} | all-to-all | bytes 2097152 | tf_op jit(solution)/shard_map/all_to_all | solution.py:21
  271.8 0.0 all-gather.5.cloned.1.call-update
  271.9 31.7 %all-gather.5.cloned.1.call-done = bf16[2048,512]{1,0:T(8,128)(2,1)} async-done(((bf16[1024,512]{1,0:T(8,128)(2,1)}), bf16[2048,512]{1,0:T(8,128)(2,1)}) %all-gather.5.cloned.1.call-update) | async-done | bytes 2097168 | tf_op jit(solution)/shard_map/all_gather | solution.py:24
  303.6 3.0 copy.32
  (22 shorter events, 0.1 us)
Async XLA Ops:
  7.2 35.5 %copy-start = (bf16[1,1,256,2048]{3,2,1,0:T(8,128)(2,1)S(1)}, bf16[1,1,256,2048]{3,2,1,0:T(8,128)(2,1)}, u32[]{:S(2)}) copy-start(bf16[1,1,256,2048]{3,2,1,0:T(8,128)(2,1)} %param.11) | copy-start | bytes 3145732
  7.2 35.4 %copy-start.6 = (s32[1,1,4,64]{3,2,1,0:T(4,128)S(1)}, s32[1,1,4,64]{3,2,1,0:T(4,128)}, u32[]{:S(2)}) copy-start(s32[1,1,4,64]{3,2,1,0:T(4,128)} %param.13) | copy-start | bytes 3076
  7.2 68.1 %all-gather.3.cloned.1.call-start = ((), (), s32[]{:S(2)}) async-start(), calls=%async_computation.3 | async-start | bytes 3145728 | tf_op jit(solution)/shard_map/all_gather | solution.py:24
  42.6 193.6 %all-reduce.3.cloned.1.call-start = ((), (), s32[]{:S(2)}) async-start(), calls=%async_computation.5 | async-start | bytes 2097152
  42.7 3.0 copy-start.9
  45.7 34.5 %copy-start.5 = (bf16[1,1,256,256]{3,2,1,0:T(8,128)(2,1)S(1)}, bf16[1,1,256,256]{3,2,1,0:T(8,128)(2,1)}, u32[]{:S(2)}) copy-start(bf16[1,1,256,256]{3,2,1,0:T(8,128)(2,1)} %param.12) | copy-start | bytes 393220
  75.2 4.4 %copy-start.1 = (bf16[2048,512]{1,0:T(8,128)(2,1)S(1)}, bf16[2048,512]{1,0:T(8,128)(2,1)}, u32[]{:S(2)}) copy-start(bf16[2048,512]{1,0:T(8,128)(2,1)} %all-gather.3.cloned.1.call-done) | copy-start | bytes 6291460
  183.5 6.7 %copy-start.7 = (s32[16]{0:T(128)S(1)}, s32[16]{0:T(128)}, u32[]{:S(2)}) copy-start(s32[16]{0:T(128)} %param.15) | copy-start | bytes 196
  190.2 7.0 %copy-start.10 = (u32[32]{0:T(128)S(1)}, u32[32]{0:T(128)}, u32[]{:S(2)}) copy-start(u32[32]{0:T(128)} %constant.58) | copy-start | bytes 388
  190.2 47.7 %copy-start.2 = (f32[4,64,512]{2,1,0:T(8,128)S(1)}, f32[4,64,512]{2,1,0:T(8,128)}, u32[]{:S(2)}) copy-start(f32[4,64,512]{2,1,0:T(8,128)} %param.17) | copy-start | bytes 1572868
  190.2 47.7 %copy-start.3 = (f32[4,64,512]{2,1,0:T(8,128)S(1)}, f32[4,64,512]{2,1,0:T(8,128)}, u32[]{:S(2)}) copy-start(f32[4,64,512]{2,1,0:T(8,128)} %param.18) | copy-start | bytes 1572868
  190.2 47.7 %copy-start.4 = (f32[4,64,512]{2,1,0:T(8,128)S(1)}, f32[4,64,512]{2,1,0:T(8,128)}, u32[]{:S(2)}) copy-start(f32[4,64,512]{2,1,0:T(8,128)} %param.19) | copy-start | bytes 1572868
  197.1 42.6 %copy-start.8 = (s32[16]{0:T(128)S(1)}, s32[16]{0:T(128)}, u32[]{:S(2)}) copy-start(s32[16]{0:T(128)} %param.16) | copy-start | bytes 196
  197.2 106.4 %all-gather.5.cloned.1.call-start = ((), (), s32[]{:S(2)}) async-start(), calls=%async_computation.4 | async-start | bytes 3145728 | tf_op jit(solution)/shard_map/all_gather | solution.py:24
Sparse Core Ops, SparseCore 0:
  42.7 32.5 all-gather.2
  197.3 38.7 all-reduce.2
  272.0 31.5 all-gather.4
where the time goes:
time: 314 us; the launch traced here: 313 us
  blocking collectives  162 us (52%)
  waiting for transfers between devices  97.6 us (31%)
  matrix products  17.4 us (6%)
  local copies, waits for them, and re-layouts  17.3 us (6%)
  between operations  14 us (4%)
  other arithmetic  4.35 us (1%)
    all_to_all x1, blocking collectives, shards(): lax.all_to_all(blocks, 'place', split_axis=1, concat_axis=1, tiled=True)  98.7 us
    all_to_all x2, blocking collectives, spread(): lax.all_to_all(picked.reshape(places, rows_shard, width), 'place', split_...  63.7 us
    all_gather x2, waiting for transfers between devices, spread(): lax.all_gather(landed.reshape(places * rows_shard, width), 'dp', axis=0,...  59.3 us
    unnamed x4, waiting for transfers between devices  38.2 us
    dot_general x1, matrix products, shards(): jnp.einsum('se,dsx->dex', select, landed.reshape(groups, places, rows_sha...  6.93 us
    reshape x1, local copies, waits for them, and re-layouts, shards(): landed.reshape(groups, places, rows_shard * width)  6.67 us
    unnamed x29, local copies, waits for them, and re-layouts  6.45 us
  transfers between devices with their start and end apart: 3, of which 3 were waited for; matrix products, arithmetic and copies ran while one was open for 2% of the time, Pallas kernels for 0%

commit v1 on v0

--- a/solution.py
+++ b/solution.py
@@ -98,6 +98,95 @@
     return (new_weights[None], new_master, new_first, new_second)
 
 
+def whole_gather(shard):
+    return lax.all_gather(shard, ("dp", "place"), axis=0, tiled=False)
+
+
+def adam(grad, master, first_moment, second_moment):
+    new_first = decay_first * first_moment + (1.0 - decay_first) * grad
+    new_second = decay_second * second_moment + (1.0 - decay_second) * grad * grad
+    first_hat = new_first / (1.0 - decay_first**step_number)
+    second_hat = new_second / (1.0 - decay_second**step_number)
+    new_master = master - learn_rate * (
+        first_hat / (jnp.sqrt(second_hat) + epsilon) + weight_decay * master
+    )
+    return new_master, new_first, new_second
+
+
+def gathered(
+    tokens,
+    hidden_grad,
+    routing,
+    row_count,
+    old_slots,
+    new_slots,
+    master,
+    first_moment,
+    second_moment,
+):
+    places = lax.axis_size("place")
+    groups = lax.axis_size("dp")
+    devices = places * groups
+    experts, rows_shard, width = master.shape
+    half = width // 2
+    place_here = lax.axis_index("place")
+    group_here = lax.axis_index("dp")
+    rows_in = tokens[0, 0]
+    rows, depth = rows_in.shape
+    order = routing[0, 0]
+    batches, batch_rows = order.shape
+    turned = rows_in.T.reshape(devices, rows_shard, rows)
+    all_weights = whole_gather(master.astype(jnp.bfloat16))
+    columns = lax.all_to_all(turned, ("dp", "place"), split_axis=0, concat_axis=0, tiled=True)
+    weights = lax.dynamic_index_in_dim(
+        all_weights, old_slots[place_here], axis=1, keepdims=False
+    ).reshape(depth, width)
+    live = jnp.arange(rows, dtype=jnp.int32) < row_count[group_here, place_here]
+    place_of = (
+        order[:, None, :] == jnp.arange(batch_rows, dtype=jnp.int32)[None, :, None]
+    ) & live.reshape(batches, 1, batch_rows)
+    incoming = jnp.einsum(
+        "mri,mik->mrk",
+        place_of.astype(jnp.bfloat16),
+        hidden_grad[0, 0].reshape(batches, batch_rows, half),
+        preferred_element_type=jnp.float32,
+    ).reshape(rows, half)
+    both = jnp.dot(rows_in, weights, preferred_element_type=jnp.float32)
+    gate = both[:, :half]
+    upward = both[:, half:]
+    sigma = jax.nn.sigmoid(gate)
+    active = gate * sigma
+    slope = sigma * (1.0 + gate * (1.0 - sigma))
+    local = jnp.concatenate([incoming * upward * slope, incoming * active], axis=1).astype(
+        jnp.bfloat16
+    )
+    all_local = whole_gather(local)
+    select = old_slots[None, :] == jnp.arange(experts, dtype=jnp.int32)[:, None]
+    chosen = jnp.tile(select, (1, groups))
+    stacked = jnp.where(
+        chosen[:, None, :, None], columns.transpose(1, 0, 2)[None], jnp.bfloat16(0)
+    ).reshape(experts * rows_shard, devices * rows)
+    grad_sum = jnp.dot(
+        stacked, all_local.reshape(devices * rows, width), preferred_element_type=jnp.float32
+    ).reshape(experts, rows_shard, width)
+    per_slot = jnp.sum(row_count.astype(jnp.float32), axis=0)
+    total = jnp.sum(jnp.where(select, per_slot[None, :], 0.0), axis=1)
+    grad = grad_sum / total[:, None, None]
+    new_master, new_first, new_second = adam(grad, master, first_moment, second_moment)
+    all_new = whole_gather(new_master.astype(jnp.bfloat16))
+    new_weights = lax.dynamic_index_in_dim(all_new, new_slots[place_here], axis=1, keepdims=True)
+    return (
+        new_weights.reshape(1, depth, width),
+        new_master,
+        new_first,
+        new_second,
+    )
+
+
+def fits(mesh):
+    return mesh.size <= 64
+
+
 def solution(mesh):
     placed = (
         P("dp", "place", None, None),
@@ -111,7 +200,7 @@
         P(None, ("dp", "place"), None),
     )
     return jax.shard_map(
-        shards,
+        gathered if fits(mesh) else shards,
         mesh=mesh,
         in_specs=placed,
         out_specs=(

time: 314 us -> 272 us (0.87)
  blocking collectives: 162 us -> 0 us
  waiting for transfers between devices: 97.6 us -> 228 us
  matrix products: 17.4 us -> 8.94 us
  local copies, waits for them, and re-layouts: 17.3 us -> 10.5 us
  between operations: 14 us -> 17.7 us
  starting transfers between devices: 0.12 us -> 3.31 us
    all_to_all x3 -> x0, blocking collectives: 162 us -> none  [the longest x1 98.7 us: shards(): lax.all_to_all(blocks, 'place', split_axis=1, concat_axis=1, tiled=True)]
    all_gather x2 -> x3, waiting for transfers between devices: 59.3 us -> 192 us  [whole_gather(): return lax.all_gather(shard, ('dp', 'place'), axis=0, tiled=False)]
    unnamed x4 -> x3, waiting for transfers between devices: 38.2 us -> 0.05 us
    all_to_all x0 -> x1, waiting for transfers between devices: none -> 36.3 us  [gathered(): lax.all_to_all(turned, ('dp', 'place'), split_axis=0, concat_axis=0, tile...]
    dot_general x12 -> x3, matrix products: 17.4 us -> 8.94 us  [the longest x1 7.34 us: gathered(): jnp.dot(stacked, all_local.reshape(devices * rows, width), preferred_elem...]
    dynamic_slice x1 -> x5, local copies, waits for them, and re-layouts: 0.59 us -> 8.06 us  [the longest x1 3.13 us: gathered(): lax.dynamic_index_in_dim(all_new, new_slots[place_here], axis=1, keepdims...]
    reshape x2 -> x1, local copies, waits for them, and re-layouts: 7.23 us -> 0.13 us  [gathered(): incoming = jnp.einsum('mri,mik->mrk', place_of.astype(jnp.bfloat16), hidd...]
    unnamed x29 -> x17, local copies, waits for them, and re-layouts: 6.45 us -> 1.36 us
  transfers between devices with their start and end apart: 3 -> 4, of which waited for: 3 -> 4; matrix products, arithmetic and copies ran while one was open for 2% -> 2% of each run, Pallas kernels for 0% -> 0%
where the time goes in v1:
time: 272 us; the launch traced here: 271 us
  waiting for transfers between devices  228 us (84%)
  between operations  17.7 us (7%)
  local copies, waits for them, and re-layouts  10.5 us (4%)
  matrix products  8.94 us (3%)
  starting transfers between devices  3.31 us (1%)
  other arithmetic  2.84 us (1%)
    all_gather x3, waiting for transfers between devices, whole_gather(): return lax.all_gather(shard, ('dp', 'place'), axis=0, tiled=False)  192 us
    all_to_all x1, waiting for transfers between devices, gathered(): lax.all_to_all(turned, ('dp', 'place'), split_axis=0, concat_axis=0, tile...  36.3 us
    dot_general x1, matrix products, gathered(): jnp.dot(stacked, all_local.reshape(devices * rows, width), preferred_elem...  7.34 us
  transfers between devices with their start and end apart: 4, of which 4 were waited for; matrix products, arithmetic and copies ran while one was open for 2% of the time, Pallas kernels for 0%

profile of v1, /device:TPU:1, one launch (start us, length us, event | category | flops | bytes accessed | tf_op | source)
XLA Modules:
  0.0 271.2 jit_solution(10125909517758947672)
XLA Ops:
  7.2 0.0 copy-start
  7.2 0.0 copy-start.1
  7.2 0.0 all-gather.8.cloned.1.call-start
  7.2 1.9 convert_element_type.18
  9.1 0.0 all-gather.8.cloned.1.call-update
  9.1 0.0 all-gather.6.cloned.1.call-start
  9.2 1.2 dynamic_slice.18
  11.7 1.3 dynamic_slice.17
  13.0 0.7 add_compare_fusion
  13.7 0.0 copy-done
  13.7 0.8 fusion.21
  14.5 0.1 copy.22
  15.3 76.2 %all-gather.8.cloned.1.call-done = bf16[128,64,512]{2,1,0:T(8,128)(2,1)} async-done(((bf16[4,64,512]{2,1,0:T(8,128)(2,1)}), bf16[128,64,512]{2,1,0:T(8,128)(2,1)}) %all-gather.8.cloned.1.call-update) | async-done | bytes 8388624 | tf_op jit(solution)/shard_map/all_gather | solution.py:102
  91.5 1.8 constant_dynamic-slice_fusion.1
  93.3 0.0 copy-done.1
  93.3 0.8 convolution_bitcast_fusion
  94.1 0.0 copy-start.6
  94.1 0.0 copy-start.3
  94.1 0.0 copy-start.2
  94.1 0.0 copy-start.4
  94.1 0.0 copy-start.5
  94.1 0.2 fusion.24
  94.3 0.8 copy.24
  95.2 0.0 all-gather.6.cloned.1.call-update
  95.2 1.3 copy.21
  96.5 3.2 %all-to-all-start = ((bf16[32,64,256]{2,1,0:T(8,128)(2,1)}), bf16[32,64,256]{2,1,0:T(8,128)(2,1)S(1)}, u32[]{:S(2)}, u32[]{:S(2)}) async-start(bf16[32,64,256]{2,1,0:T(8,128)(2,1)} %bitcast.2), calls=%async_computation | async-start | bytes 2097152 | tf_op jit(solution)/shard_map/all_to_all | solution.py:140
  99.7 0.0 all-gather.10.cloned.1.call-start
  99.7 0.0 copy-done.6
  99.8 0.1 tile.9
  99.9 0.0 copy-done.3
  99.9 0.1 select_reduce_fusion
  100.0 36.3 %all-to-all-done = bf16[32,64,256]{2,1,0:T(8,128)(2,1)S(1)} async-done(((bf16[32,64,256]{2,1,0:T(8,128)(2,1)}), bf16[32,64,256]{2,1,0:T(8,128)(2,1)S(1)}, u32[]{:S(2)}, u32[]{:S(2)}) %all-to-all-start) | async-done | bytes 1048608 | tf_op jit(solution)/shard_map/all_to_all | solution.py:140
  136.3 41.7 %all-gather.6.cloned.1.call-done = bf16[32,256,512]{2,1,0:T(8,128)(2,1)} async-done(((bf16[1,256,512]{2,1,0:T(8,128)(2,1)}), bf16[32,256,512]{2,1,0:T(8,128)(2,1)}) %all-gather.6.cloned.1.call-update) | async-done | bytes 8388624 | tf_op jit(solution)/shard_map/all_gather | solution.py:102
  177.9 0.0 copy-done.2
  177.9 0.0 copy-done.4
  177.9 0.0 copy-done.5
  178.0 0.0 copy-start.7
  178.0 7.3 %fusion.28 = (bf16[4,64,512]{2,1,0:T(8,128)(2,1)}, f32[4,64,512]{2,1,0:T(8,128)}, f32[4,64,512]{2,1,0:T(8,128)}, f32[4,64,512]{2,1,0:T(8,128)}) fusion(f32[4,64,512]{2,1,0:T(8,128)S(1)} %copy-done.2, f32[4,64,512]{2,1,0:T(8,128)S(1)} %copy-done.4, f32[4,64,512]{2,1,0:T(8,128)S(1)} %copy-done.5, f32[4]{0:T(128)S(1)} %select_reduce_fusion, ...), kind=kOutput, calls=%fused_computation.34 | convolution fusion | flops 2151809024 | bytes 12845200 | tf_op jit(solution)/shard_map/dot_general | solution.py:169
  185.3 0.0 all-gather.10.cloned.1.call-update
  185.3 0.0 copy-done.7
  185.3 0.6 dynamic_slice.20
  187.8 73.7 %all-gather.10.cloned.1.call-done = bf16[128,64,512]{2,1,0:T(8,128)(2,1)} async-done(((bf16[4,64,512]{2,1,0:T(8,128)(2,1)}), bf16[128,64,512]{2,1,0:T(8,128)(2,1)}) %all-gather.10.cloned.1.call-update) | async-done | bytes 8388624 | tf_op jit(solution)/shard_map/all_gather | solution.py:102
  261.6 3.1 %constant_dynamic-slice_fusion = bf16[32,1,64,512]{3,2,1,0:T(8,128)(2,1)} fusion(bf16[32,4,64,512]{3,2,1,0:T(8,128)(2,1)} %bitcast.47, s32[]{:T(128)S(6)} %select_n.32), kind=kLoop, calls=%fused_computation.31 | loop fusion | bytes 4194308 | tf_op jit(solution)/shard_map/jit(dynamic_index_in_dim)/dynamic_slice | solution.py:177
  (4 shorter events, 0.1 us)
Async XLA Ops:
  7.2 6.5 %copy-start = (bf16[1,1,256,256]{3,2,1,0:T(8,128)(2,1)S(1)}, bf16[1,1,256,256]{3,2,1,0:T(8,128)(2,1)}, u32[]{:S(2)}) copy-start(bf16[1,1,256,256]{3,2,1,0:T(8,128)(2,1)} %param.10) | copy-start | bytes 393220
  7.2 86.1 %copy-start.1 = (bf16[1,1,256,2048]{3,2,1,0:T(8,128)(2,1)S(1)}, bf16[1,1,256,2048]{3,2,1,0:T(8,128)(2,1)}, u32[]{:S(2)}) copy-start(bf16[1,1,256,2048]{3,2,1,0:T(8,128)(2,1)} %param.9) | copy-start | bytes 3145732
  7.2 84.3 %all-gather.8.cloned.1.call-start = ((), (), s32[]{:S(2)}) async-start(), calls=%async_computation.2 | async-start | bytes 8650752 | tf_op jit(solution)/shard_map/all_gather | solution.py:102
  9.1 168.8 %all-gather.6.cloned.1.call-start = ((), (), s32[]{:S(2)}) async-start(), calls=%async_computation.1 | async-start | bytes 8650752 | tf_op jit(solution)/shard_map/all_gather | solution.py:102
  94.1 5.7 %copy-start.6 = (s32[16]{0:T(128)S(1)}, s32[16]{0:T(128)}, u32[]{:S(2)}) copy-start(s32[16]{0:T(128)} %param.13) | copy-start | bytes 196
  94.1 5.8 %copy-start.3 = (s32[2,16]{1,0:T(2,128)S(1)}, s32[2,16]{1,0:T(2,128)}, u32[]{:S(2)}) copy-start(s32[2,16]{1,0:T(2,128)} %param.12) | copy-start | bytes 388
  94.1 83.9 %copy-start.2 = (f32[4,64,512]{2,1,0:T(8,128)S(1)}, f32[4,64,512]{2,1,0:T(8,128)}, u32[]{:S(2)}) copy-start(f32[4,64,512]{2,1,0:T(8,128)} %param.15) | copy-start | bytes 1572868
  94.1 83.9 %copy-start.4 = (f32[4,64,512]{2,1,0:T(8,128)S(1)}, f32[4,64,512]{2,1,0:T(8,128)}, u32[]{:S(2)}) copy-start(f32[4,64,512]{2,1,0:T(8,128)} %param.16) | copy-start | bytes 1572868
  94.1 83.8 %copy-start.5 = (f32[4,64,512]{2,1,0:T(8,128)S(1)}, f32[4,64,512]{2,1,0:T(8,128)}, u32[]{:S(2)}) copy-start(f32[4,64,512]{2,1,0:T(8,128)} %param.17) | copy-start | bytes 1572868
  96.5 39.8 %all-to-all-start = ((bf16[32,64,256]{2,1,0:T(8,128)(2,1)}), bf16[32,64,256]{2,1,0:T(8,128)(2,1)S(1)}, u32[]{:S(2)}, u32[]{:S(2)}) async-start(bf16[32,64,256]{2,1,0:T(8,128)(2,1)} %bitcast.2), calls=%async_computation | async-start | bytes 2097152 | tf_op jit(solution)/shard_map/all_to_all | solution.py:140
  99.7 161.9 %all-gather.10.cloned.1.call-start = ((), (), s32[]{:S(2)}) async-start(), calls=%async_computation.3 | async-start | bytes 8650752 | tf_op jit(solution)/shard_map/all_gather | solution.py:102
  178.0 7.4 %copy-start.7 = (s32[16]{0:T(128)S(1)}, s32[16]{0:T(128)}, u32[]{:S(2)}) copy-start(s32[16]{0:T(128)} %param.14) | copy-start | bytes 196
Sparse Core Ops, SparseCore 0:
  11.4 79.9 all-gather.7
  95.3 82.5 all-gather.5
  185.4 76.0 all-gather.9

commit v2 on v1

--- a/solution.py
+++ b/solution.py
@@ -1,6 +1,10 @@
+import functools
+
 import jax
 import jax.numpy as jnp
 from jax import lax
+from jax.experimental import pallas as pl
+from jax.experimental.pallas import tpu as pltpu
 from jax.sharding import PartitionSpec as P
 
 decay_first = 0.9
@@ -98,8 +102,108 @@
     return (new_weights[None], new_master, new_first, new_second)
 
 
+MESH = pl.DeviceIdType.MESH
+
+
+def route(groups, places):
+    here = lax.axis_index("place")
+    return lax.axis_index("dp"), here // 4, (here // 2) % 2, here % 2
+
+
+def gather_kernel(groups, places, own_ref, all_ref, send_sem, recv_sem, own_sem):
+    levels = places // 4
+    y, z, x, c = route(groups, places)
+
+    def block(y, z, x, c):
+        return y * places + z * 4 + x * 2 + c
+
+    def device(y, z, x, c):
+        return (y, z * 4 + x * 2 + c)
+
+    x_first, y_first = (x + 1 - c) % 2, (y + c) % 2
+    x_last, y_last = (x + c) % 2, (y + 1 - c) % 2
+    lines = [device(y, (z + k) % levels, x, c) for k in range(1, levels)]
+    first = device(y_first, z, x_first, c)
+    last = device(y_last, z, x_last, c)
+    sibling = device(y, z, x, 1 - c)
+    partners = lines + [first, last, sibling]
+
+    barrier = pltpu.get_barrier_semaphore()
+    for partner in partners:
+        pl.semaphore_signal(barrier, inc=1, device_id=partner, device_id_type=MESH)
+    pl.semaphore_wait(barrier, len(partners))
+
+    mine = block(y, z, x, c)
+    sends = []
+
+    def send(index, partner, source=None):
+        copy = pltpu.make_async_remote_copy(
+            src_ref=all_ref.at[index] if source is None else source,
+            dst_ref=all_ref.at[index],
+            send_sem=send_sem.at[len(sends)],
+            recv_sem=recv_sem.at[index],
+            device_id=partner,
+            device_id_type=MESH,
+        )
+        copy.start()
+        sends.append(copy)
+
+    def arrived(index):
+        pltpu.make_async_remote_copy(
+            src_ref=all_ref.at[index],
+            dst_ref=all_ref.at[index],
+            send_sem=send_sem.at[0],
+            recv_sem=recv_sem.at[index],
+            device_id=sibling,
+            device_id_type=MESH,
+        ).wait_recv()
+
+    for partner in (first, last, *lines, sibling):
+        send(mine, partner, own_ref)
+    keep = pltpu.make_async_copy(own_ref, all_ref.at[mine], own_sem)
+    keep.start()
+    for k in range(levels):
+        level = (z + k) % levels
+        if k:
+            straight = block(y, level, x, c)
+            arrived(straight)
+            for partner in (first, last, sibling):
+                send(straight, partner)
+        over = block(y_first, level, x_first, c)
+        arrived(over)
+        for partner in (last, sibling):
+            send(over, partner)
+    for k in range(levels):
+        level = (z + k) % levels
+        for index in (block(y_last, level, x_last, c), block(1 - y, level, 1 - x, c)):
+            arrived(index)
+            send(index, sibling)
+    for k in range(levels):
+        level = (z + k) % levels
+        for side in range(2):
+            for group in range(2):
+                arrived(block(group, level, side, 1 - c))
+    keep.wait()
+    for copy in sends:
+        copy.wait_send()
+
+
 def whole_gather(shard):
-    return lax.all_gather(shard, ("dp", "place"), axis=0, tiled=False)
+    places = lax.axis_size("place")
+    groups = lax.axis_size("dp")
+    devices = groups * places
+    return pl.pallas_call(
+        functools.partial(gather_kernel, groups, places),
+        out_shape=jax.ShapeDtypeStruct((devices,) + shard.shape, shard.dtype),
+        in_specs=[pl.BlockSpec(memory_space=pl.ANY)],
+        out_specs=pl.BlockSpec(memory_space=pl.ANY),
+        scratch_shapes=[
+            pltpu.SemaphoreType.DMA((devices,)),
+            pltpu.SemaphoreType.DMA((devices,)),
+            pltpu.SemaphoreType.DMA,
+        ],
+        compiler_params=pltpu.CompilerParams(collective_id=0, has_side_effects=True),
+    )(shard)
 
 
 def adam(grad, master, first_moment, second_moment):
@@ -160,7 +264,7 @@
     local = jnp.concatenate([incoming * upward * slope, incoming * active], axis=1).astype(
         jnp.bfloat16
     )
-    all_local = whole_gather(local)
+    all_local = whole_gather(local.reshape(experts, rows * width // (experts * width), width))
     select = old_slots[None, :] == jnp.arange(experts, dtype=jnp.int32)[:, None]
     chosen = jnp.tile(select, (1, groups))
     stacked = jnp.where(
@@ -184,7 +288,7 @@
 
 
 def fits(mesh):
-    return mesh.size <= 64
+    return mesh.shape["dp"] == 2 and mesh.shape["place"] in (4, 8, 16)
 
 
 def solution(mesh):

time: 272 us -> 225 us (0.83)
  the two profiles are of different devices: /device:TPU:1 before, /device:TPU:9 now
where the time goes in v2:
time: 225 us; the launch traced here: 224 us
  Pallas kernels  193 us (86%)
  local copies, waits for them, and re-layouts  9.39 us (4%)
  matrix products  8.15 us (4%)
  starting transfers between devices  6.36 us (3%)
  between operations  4.85 us (2%)
  other arithmetic  2.39 us (1%)
    pallas_call x3, Pallas kernels, whole_gather(): pl.pallas_call(functools.partial(gather_kernel, groups, places), out_shap...  193 us
    dot_general x1, matrix products, gathered(): jnp.dot(stacked, all_local.reshape(devices * rows, width), preferred_elem...  7.29 us
    all_to_all x1, starting transfers between devices, gathered(): lax.all_to_all(turned, ('dp', 'place'), split_axis=0, concat_axis=0, tile...  6.36 us
  transfers between devices with their start and end apart: 1, of which 0 were waited for; matrix products, arithmetic and copies ran while one was open for 3% of the time, Pallas kernels for 60%

profile of v2, /device:TPU:9, one launch (start us, length us, event | category | flops | bytes accessed | tf_op | source)
XLA Modules:
  0.0 224.2 jit_solution(9669703162185580821)
XLA Ops:
  0.6 0.0 copy-start
  0.6 0.0 copy-start.8
  0.7 0.0 copy-start.7
  0.7 0.0 copy-start.2
  0.7 2.3 %copy.13 = bf16[1,1,256,2048]{2,3,1,0:T(8,128)(2,1)} copy(bf16[1,1,256,2048]{3,2,1,0:T(8,128)(2,1)} %param.9) | data formatting | bytes 2097152 | tf_op args[0]
  3.0 6.4 %all-to-all-start = ((bf16[32,64,256]{2,1,0:T(8,128)(2,1)}), bf16[32,64,256]{2,1,0:T(8,128)(2,1)S(1)}, u32[]{:S(2)}, u32[]{:S(2)}) async-start(bf16[32,64,256]{2,1,0:T(8,128)(2,1)} %bitcast.2), calls=%async_computation | async-start | bytes 2097152 | tf_op jit(solution)/shard_map/all_to_all | solution.py:244
  9.4 0.0 copy-done.8
  9.4 0.6 dynamic_slice.18
  11.3 0.0 copy-done.7
  11.3 0.6 dynamic_slice.20
  13.2 0.1 tile.9
  13.3 0.1 broadcast_bitcast_fusion
  13.4 0.0 copy-done.2
  13.4 0.7 convert_element_type.12.own_ref
  14.2 0.0 copy-start.4
  14.2 76.4 %shard_map.120 = bf16[32,4,64,512]{3,2,1,0:T(8,128)(2,1)} custom-call(bf16[4,64,512]{2,1,0:T(8,128)(2,1)} %convert_element_type.12.own_ref), custom_call_target="tpu_custom_call" | custom-call | tf_op jit(solution)/shard_map/pallas_call | solution.py:195
  90.6 0.0 copy-start.3
  90.6 0.0 copy-start.1
  91.4 0.0 copy-done.4
  91.4 0.6 dynamic_slice.17
  92.0 0.7 add_compare_fusion
  92.6 1.8 constant_dynamic-slice_fusion.1
  94.5 0.0 copy-done
  94.5 0.0 copy-done.3
  94.5 0.2 fusion.14
  94.6 0.0 copy-done.1
  94.7 0.7 convolution_bitcast_fusion
  95.4 0.1 fusion.11
  95.5 0.7 pad_maximum_fusion.own_ref
  96.2 0.0 copy-start.5
  96.2 0.0 copy-start.6
  96.2 57.1 %shard_map.121 = bf16[32,4,64,512]{3,2,1,0:T(8,128)(2,1)} custom-call(bf16[4,64,512]{2,1,0:T(8,128)(2,1)} %pad_maximum_fusion.own_ref), custom_call_target="tpu_custom_call" | custom-call | tf_op jit(solution)/shard_map/pallas_call | solution.py:195
  154.0 0.1 select_reduce_fusion
  154.1 0.0 all-to-all-done
  154.1 0.1 copy.15
  154.2 0.0 copy-done.5
  154.2 0.0 copy-done.6
  154.2 7.3 %fusion.19 = (bf16[4,64,512]{2,1,0:T(8,128)(2,1)}, f32[4,64,512]{2,1,0:T(8,128)}, f32[4,64,512]{2,1,0:T(8,128)}, f32[4,64,512]{2,1,0:T(8,128)}) fusion(f32[4,64,512]{2,1,0:T(8,128)S(1)} %copy-done.2, f32[4,64,512]{2,1,0:T(8,128)S(1)} %copy-done.5, f32[4,64,512]{2,1,0:T(8,128)S(1)} %copy-done.6, f32[4]{0:T(128)S(1)} %select_reduce_fusion, ...), kind=kOutput, calls=%fused_computation.32 | convolution fusion | flops 2151809024 | bytes 12877840 | tf_op jit(solution)/shard_map/dot_general | solution.py:273
  161.5 59.5 %shard_map.122 = bf16[32,4,64,512]{3,2,1,0:T(8,128)(2,1)} custom-call(bf16[4,64,512]{2,1,0:T(8,128)(2,1)} %get-tuple-element.4.own_ref), custom_call_target="tpu_custom_call" | custom-call | tf_op jit(solution)/shard_map/pallas_call | solution.py:195
  221.0 3.1 %constant_dynamic-slice_fusion = bf16[32,1,64,512]{3,2,1,0:T(8,128)(2,1)} fusion(bf16[32,4,64,512]{3,2,1,0:T(8,128)(2,1)} %shard_map.122, s32[]{:T(128)S(6)} %select_n.33), kind=kLoop, calls=%fused_computation.29 | loop fusion | bytes 4194308 | tf_op jit(solution)/shard_map/jit(dynamic_index_in_dim)/dynamic_slice | solution.py:281
  (4 shorter events, 0.1 us)
Async XLA Ops:
  0.6 93.8 %copy-start = (bf16[1,1,256,256]{3,2,1,0:T(8,128)(2,1)S(1)}, bf16[1,1,256,256]{3,2,1,0:T(8,128)(2,1)}, u32[]{:S(2)}) copy-start(bf16[1,1,256,256]{3,2,1,0:T(8,128)(2,1)} %param.10) | copy-start | bytes 393220
  0.6 8.7 %copy-start.8 = (s32[16]{0:T(128)S(1)}, s32[16]{0:T(128)}, u32[]{:S(2)}) copy-start(s32[16]{0:T(128)} %param.13) | copy-start | bytes 196
  0.7 10.6 %copy-start.7 = (s32[16]{0:T(128)S(1)}, s32[16]{0:T(128)}, u32[]{:S(2)}) copy-start(s32[16]{0:T(128)} %param.14) | copy-start | bytes 196
  0.7 12.8 %copy-start.2 = (f32[4,64,512]{2,1,0:T(8,128)S(1)}, f32[4,64,512]{2,1,0:T(8,128)}, u32[]{:S(2)}) copy-start(f32[4,64,512]{2,1,0:T(8,128)} %param.15) | copy-start | bytes 1572868
  3.0 151.1 %all-to-all-start = ((bf16[32,64,256]{2,1,0:T(8,128)(2,1)}), bf16[32,64,256]{2,1,0:T(8,128)(2,1)S(1)}, u32[]{:S(2)}, u32[]{:S(2)}) async-start(bf16[32,64,256]{2,1,0:T(8,128)(2,1)} %bitcast.2), calls=%async_computation | async-start | bytes 2097152 | tf_op jit(solution)/shard_map/all_to_all | solution.py:244
  14.2 77.2 %copy-start.4 = (s32[2,16]{1,0:T(2,128)S(1)}, s32[2,16]{1,0:T(2,128)}, u32[]{:S(2)}) copy-start(s32[2,16]{1,0:T(2,128)} %param.12) | copy-start | bytes 388
  90.6 3.9 %copy-start.3 = (s32[1,1,4,64]{3,2,1,0:T(4,128)S(1)}, s32[1,1,4,64]{3,2,1,0:T(4,128)}, u32[]{:S(2)}) copy-start(s32[1,1,4,64]{3,2,1,0:T(4,128)} %param.11) | copy-start | bytes 3076
  90.6 4.0 %copy-start.1 = (bf16[1,1,256,2048]{3,2,1,0:T(8,128)(2,1)S(1)}, bf16[1,1,256,2048]{3,2,1,0:T(8,128)(2,1)}, u32[]{:S(2)}) copy-start(bf16[1,1,256,2048]{3,2,1,0:T(8,128)(2,1)} %param.9) | copy-start | bytes 3145732
  96.2 58.0 %copy-start.5 = (f32[4,64,512]{2,1,0:T(8,128)S(1)}, f32[4,64,512]{2,1,0:T(8,128)}, u32[]{:S(2)}) copy-start(f32[4,64,512]{2,1,0:T(8,128)} %param.16) | copy-start | bytes 1572868
  96.2 58.0 %copy-start.6 = (f32[4,64,512]{2,1,0:T(8,128)S(1)}, f32[4,64,512]{2,1,0:T(8,128)}, u32[]{:S(2)}) copy-start(f32[4,64,512]{2,1,0:T(8,128)} %param.17) | copy-start | bytes 1572868

commit v3 on v1

--- a/solution.py
+++ b/solution.py
@@ -1,6 +1,10 @@
+import functools
+
 import jax
 import jax.numpy as jnp
 from jax import lax
+from jax.experimental import pallas as pl
+from jax.experimental.pallas import tpu as pltpu
 from jax.sharding import PartitionSpec as P
 
 decay_first = 0.9
@@ -98,8 +102,238 @@
     return (new_weights[None], new_master, new_first, new_second)
 
 
+MESH = pl.DeviceIdType.MESH
+
+
+def spot(places):
+    here = lax.axis_index("place")
+    return lax.axis_index("dp"), here // 4, (here // 2) % 2, here % 2
+
+
+def device(y, z, x, c):
+    return (y, z * 4 + x * 2 + c)
+
+
+def meet(partners, z, levels, up, down):
+    barrier = pltpu.get_barrier_semaphore()
+
+    def greet(partner):
+        pl.semaphore_signal(barrier, inc=1, device_id=partner, device_id_type=MESH)
+
+    for partner in partners:
+        greet(partner)
+    pl.when(z < levels - 1)(lambda: greet(up))
+    pl.when(z > 0)(lambda: greet(down))
+    has_down = (z + levels - 2) // (levels - 1)
+    has_up = (2 * levels - 3 - z) // (levels - 1)
+    pl.semaphore_wait(barrier, len(partners) + has_up + has_down)
+
+
+def remote(source, target, send_sem, recv_sem, partner):
+    return pltpu.make_async_remote_copy(
+        src_ref=source,
+        dst_ref=target,
+        send_sem=send_sem,
+        recv_sem=recv_sem,
+        device_id=partner,
+        device_id_type=MESH,
+    )
+
+
+def gather_kernel(places, own_ref, all_ref, send_sem, recv_sem, own_sem):
+    levels = places // 4
+    y, z, x, c = spot(places)
+
+    def block(y, z, x, c):
+        return y * places + z * 4 + x * 2 + c
+
+    x_first, y_first = (x + 1 - c) % 2, (y + c) % 2
+    x_last, y_last = (x + c) % 2, (y + 1 - c) % 2
+    up, down = device(y, z + 1, x, c), device(y, z - 1, x, c)
+    first = device(y_first, z, x_first, c)
+    last = device(y_last, z, x_last, c)
+    sibling = device(y, z, x, 1 - c)
+    meet([first, last, sibling], z, levels, up, down)
+
+    def copy(kind, level, index, partner, source=None):
+        return remote(
+            all_ref.at[index] if source is None else source,
+            all_ref.at[index],
+            send_sem.at[kind, level],
+            recv_sem.at[index],
+            partner,
+        )
+
+    def arrived(index):
+        copy(0, 0, index, sibling).wait_recv()
+
+    mine = block(y, z, x, c)
+    pl.when(z < levels - 1)(lambda: copy(0, z, mine, up, own_ref).start())
+    pl.when(z > 0)(lambda: copy(1, z, mine, down, own_ref).start())
+    copy(2, z, mine, first, own_ref).start()
+    copy(3, z, mine, last, own_ref).start()
+    copy(4, z, mine, sibling, own_ref).start()
+    keep = pltpu.make_async_copy(own_ref, all_ref.at[mine], own_sem)
+    keep.start()
+
+    def straight(level, below):
+        index = block(y, level, x, c)
+        arrived(index)
+        if below:
+            pl.when(z < levels - 1)(lambda: copy(0, level, index, up).start())
+        else:
+            pl.when(z > 0)(lambda: copy(1, level, index, down).start())
+        copy(2, level, index, first).start()
+        copy(3, level, index, last).start()
+        copy(4, level, index, sibling).start()
+
+    def over(level, below):
+        index = block(y_first, level, x_first, c)
+        arrived(index)
+        copy(5, level, index, last).start()
+        copy(6, level, index, sibling).start()
+
+    def both_ways(k, visit):
+        if k == 0:
+            visit(z, True)
+        else:
+            pl.when(z >= k)(lambda: visit(z - k, True))
+            pl.when(z < levels - k)(lambda: visit(z + k, False))
+
+    for k in range(1, levels):
+        both_ways(k, straight)
+        both_ways(k - 1, over)
+    both_ways(levels - 1, over)
+
+    def ending(level, below):
+        for kind, index in ((7, block(y_last, level, x_last, c)), (8, block(1 - y, level, 1 - x, c))):
+            arrived(index)
+            copy(kind, level, index, sibling).start()
+
+    for k in range(levels):
+        both_ways(k, ending)
+    for level in range(levels):
+        for side in range(2):
+            for group in range(2):
+                arrived(block(group, level, side, 1 - c))
+    keep.wait()
+    for level in range(levels):
+        for kind in range(2, 9):
+            copy(kind, level, mine, sibling).wait_send()
+        pl.when((z >= level) & (z < levels - 1))(
+            lambda level=level: copy(0, level, mine, sibling).wait_send()
+        )
+        pl.when((z <= level) & (z > 0))(
+            lambda level=level: copy(1, level, mine, sibling).wait_send()
+        )
+
+
 def whole_gather(shard):
-    return lax.all_gather(shard, ("dp", "place"), axis=0, tiled=False)
+    places = lax.axis_size("place")
+    devices = lax.axis_size("dp") * places
+    levels = places // 4
+    return pl.pallas_call(
+        functools.partial(gather_kernel, places),
+        out_shape=jax.ShapeDtypeStruct((devices,) + shard.shape, shard.dtype),
+        in_specs=[pl.BlockSpec(memory_space=pl.ANY)],
+        out_specs=pl.BlockSpec(memory_space=pl.ANY),
+        scratch_shapes=[
+            pltpu.SemaphoreType.DMA((9, levels)),
+            pltpu.SemaphoreType.DMA((devices,)),
+            pltpu.SemaphoreType.DMA,
+        ],
+        compiler_params=pltpu.CompilerParams(collective_id=0, has_side_effects=True),
+    )(shard)
+
+
+def expert_kernel(
+    places, slots_ref, own_ref, out_ref, line, held, picked, line_send, line_recv, send_sem, recv_sem
+):
+    levels = places // 4
+    y, z, x, c = spot(places)
+    up, down = device(y, z + 1, x, c), device(y, z - 1, x, c)
+    shifts = [(0, 1, 0), (1, 0, 0), (0, 1, 1), (1, 0, 1), (1, 1, 0), (1, 1, 1), (0, 0, 1)]
+    plane = [((y + dy) % 2, (x + dx) % 2, (c + dc) % 2) for dy, dx, dc in shifts]
+    partners = [device(there_y, z, there_x, there_c) for there_y, there_x, there_c in plane]
+    line[z] = own_ref[...]
+    meet(partners, z, levels, up, down)
+
+    def pass_on(way, level):
+        return remote(
+            line.at[level],
+            line.at[level],
+            line_send.at[way, level],
+            line_recv.at[level],
+            (up, down)[way],
+        )
+
+    def hand(j, level, index):
+        return remote(
+            picked.at[j, level],
+            out_ref.at[index],
+            send_sem.at[j, level],
+            recv_sem.at[index],
+            partners[j],
+        )
+
+    def fan(level):
+        index = y * places + level * 4 + x * 2 + c
+        held[...] = line[level]
+        for j, partner in enumerate(partners):
+            picked[j, level] = held[slots_ref[partner[1]]]
+            hand(j, level, index).start()
+        out_ref[index] = held[slots_ref[z * 4 + x * 2 + c]]
+
+    pl.when(z < levels - 1)(lambda: pass_on(0, z).start())
+    pl.when(z > 0)(lambda: pass_on(1, z).start())
+    fan(z)
+
+    def below(level):
+        pass_on(0, level).wait_recv()
+        pl.when(z < levels - 1)(lambda: pass_on(0, level).start())
+        fan(level)
+
+    def above(level):
+        pass_on(1, level).wait_recv()
+        pl.when(z > 0)(lambda: pass_on(1, level).start())
+        fan(level)
+
+    for k in range(1, levels):
+        pl.when(z >= k)(lambda k=k: below(z - k))
+        pl.when(z < levels - k)(lambda k=k: above(z + k))
+    for level in range(levels):
+        for j, (there_y, there_x, there_c) in enumerate(plane):
+            hand(j, level, there_y * places + level * 4 + there_x * 2 + there_c).wait()
+        pl.when((z >= level) & (z < levels - 1))(lambda level=level: pass_on(0, level).wait_send())
+        pl.when((z <= level) & (z > 0))(lambda level=level: pass_on(1, level).wait_send())
+
+
+def expert_rows(shard, slots):
+    places = lax.axis_size("place")
+    devices = lax.axis_size("dp") * places
+    levels = places // 4
+    tile = shard.shape[1:]
+    return pl.pallas_call(
+        functools.partial(expert_kernel, places),
+        out_shape=jax.ShapeDtypeStruct((devices,) + tile, shard.dtype),
+        in_specs=[
+            pl.BlockSpec(memory_space=pltpu.SMEM),
+            pl.BlockSpec(memory_space=pltpu.VMEM),
+        ],
+        out_specs=pl.BlockSpec(memory_space=pltpu.VMEM),
+        scratch_shapes=[
+            pltpu.VMEM((levels,) + shard.shape, shard.dtype),
+            pltpu.VMEM(shard.shape, shard.dtype),
+            pltpu.VMEM((7, levels) + tile, shard.dtype),
+            pltpu.SemaphoreType.DMA((2, levels)),
+            pltpu.SemaphoreType.DMA((levels,)),
+            pltpu.SemaphoreType.DMA((7, levels)),
+            pltpu.SemaphoreType.DMA((devices,)),
+        ],
+        compiler_params=pltpu.CompilerParams(
+            collective_id=1, has_side_effects=True, vmem_limit_bytes=32 * 2**20
+        ),
+    )(slots, shard)
 
 
 def adam(grad, master, first_moment, second_moment):
@@ -136,11 +370,8 @@
     order = routing[0, 0]
     batches, batch_rows = order.shape
     turned = rows_in.T.reshape(devices, rows_shard, rows)
-    all_weights = whole_gather(master.astype(jnp.bfloat16))
     columns = lax.all_to_all(turned, ("dp", "place"), split_axis=0, concat_axis=0, tiled=True)
-    weights = lax.dynamic_index_in_dim(
-        all_weights, old_slots[place_here], axis=1, keepdims=False
-    ).reshape(depth, width)
+    weights = expert_rows(master.astype(jnp.bfloat16), old_slots).reshape(depth, width)
     live = jnp.arange(rows, dtype=jnp.int32) < row_count[group_here, place_here]
     place_of = (
         order[:, None, :] == jnp.arange(batch_rows, dtype=jnp.int32)[None, :, None]
@@ -160,7 +391,7 @@
     local = jnp.concatenate([incoming * upward * slope, incoming * active], axis=1).astype(
         jnp.bfloat16
     )
-    all_local = whole_gather(local)
+    all_local = whole_gather(local.reshape(experts, rows * width // (experts * width), width))
     select = old_slots[None, :] == jnp.arange(experts, dtype=jnp.int32)[:, None]
     chosen = jnp.tile(select, (1, groups))
     stacked = jnp.where(
@@ -173,8 +404,7 @@
     total = jnp.sum(jnp.where(select, per_slot[None, :], 0.0), axis=1)
     grad = grad_sum / total[:, None, None]
     new_master, new_first, new_second = adam(grad, master, first_moment, second_moment)
-    all_new = whole_gather(new_master.astype(jnp.bfloat16))
-    new_weights = lax.dynamic_index_in_dim(all_new, new_slots[place_here], axis=1, keepdims=True)
+    new_weights = expert_rows(new_master.astype(jnp.bfloat16), new_slots)
     return (
         new_weights.reshape(1, depth, width),
         new_master,
@@ -184,7 +414,7 @@
 
 
 def fits(mesh):
-    return mesh.size <= 64
+    return mesh.shape["dp"] == 2 and mesh.shape["place"] in (8, 16)
 
 
 def solution(mesh):

time: 272 us -> 148 us (0.54)
  waiting for transfers between devices: 228 us -> 0.01 us
  Pallas kernels: 0 us -> 124 us
  between operations: 17.7 us -> 0.85 us
  local copies, waits for them, and re-layouts: 10.5 us -> 4.57 us
  starting transfers between devices: 3.31 us -> 7.1 us
    all_gather x3 -> x0, waiting for transfers between devices: 192 us -> none  [whole_gather(): return lax.all_gather(shard, ('dp', 'place'), axis=0, tiled=False)]
    pallas_call x0 -> x3, Pallas kernels: none -> 124 us  [the longest x2 83.5 us: expert_rows(): pl.pallas_call(functools.partial(expert_kernel, places), out_shape=jax.Sh...]
    all_to_all x1, waiting for transfers between devices: 36.3 us -> 0.01 us  [gathered(): lax.all_to_all(turned, ('dp', 'place'), split_axis=0, concat_axis=0, tile...]
    dynamic_slice x4 -> x0, local copies, waits for them, and re-layouts: 6.79 us -> none  [the longest x1 3.13 us: gathered(): lax.dynamic_index_in_dim(all_new, new_slots[place_here], axis=1, keepdims...]
    all_to_all x1, starting transfers between devices: 3.19 us -> 7.1 us  [gathered(): lax.all_to_all(turned, ('dp', 'place'), split_axis=0, concat_axis=0, tile...]
  transfers between devices with their start and end apart: 4 -> 1, of which waited for: 4 -> 0; matrix products, arithmetic and copies ran while one was open for 2% -> 3% of each run, Pallas kernels for 0% -> 64%
where the time goes in v3:
time: 148 us
  Pallas kernels  124 us (84%)
  matrix products  9.36 us (6%)
  starting transfers between devices  7.1 us (5%)
  local copies, waits for them, and re-layouts  4.57 us (3%)
  other arithmetic  1.69 us (1%)
    pallas_call x2, Pallas kernels, expert_rows(): pl.pallas_call(functools.partial(expert_kernel, places), out_shape=jax.Sh...  83.5 us
    pallas_call x1, Pallas kernels, whole_gather(): pl.pallas_call(functools.partial(gather_kernel, places), out_shape=jax.Sh...  40.7 us
    dot_general x1, matrix products, gathered(): jnp.dot(stacked, all_local.reshape(devices * rows, width), preferred_elem...  7.24 us
    all_to_all x1, starting transfers between devices, gathered(): lax.all_to_all(turned, ('dp', 'place'), split_axis=0, concat_axis=0, tile...  7.1 us
    unnamed x22, local copies, waits for them, and re-layouts  3.82 us
  transfers between devices with their start and end apart: 1, of which 0 were waited for; matrix products, arithmetic and copies ran while one was open for 3% of the time, Pallas kernels for 64%

profile of v3, /device:TPU:1, one launch (start us, length us, event | category | flops | bytes accessed | tf_op | source)
XLA Modules:
  0.0 147.8 jit_solution(8682099872347710291)
XLA Ops:
  0.6 0.0 copy-start
  0.6 0.0 copy-start.1
  0.7 0.0 copy-start.3
  0.7 0.0 copy-start.6
  0.7 0.0 copy-start.5
  0.7 2.3 %copy.13 = bf16[1,1,256,2048]{2,3,1,0:T(8,128)(2,1)} copy(bf16[1,1,256,2048]{3,2,1,0:T(8,128)(2,1)} %param.9) | data formatting | bytes 2097152 | tf_op args[0]
  3.0 7.1 %all-to-all-start = ((bf16[32,64,256]{2,1,0:T(8,128)(2,1)}), bf16[32,64,256]{2,1,0:T(8,128)(2,1)S(1)}, u32[]{:S(2)}, u32[]{:S(2)}) async-start(bf16[32,64,256]{2,1,0:T(8,128)(2,1)} %bitcast.2), calls=%async_computation | async-start | bytes 2097152 | tf_op jit(solution)/shard_map/all_to_all | solution.py:373
  10.1 0.0 copy-done.1
  10.2 0.1 tile.9
  10.2 0.1 broadcast_bitcast_fusion
  10.4 0.0 copy-done.3
  10.4 53.2 %shard_map.120 = bf16[32,64,512]{2,1,0:T(8,128)(2,1)S(1)} custom-call(s32[16]{0:T(128)S(1)} %copy-done.1, bf16[4,64,512]{2,1,0:T(8,128)(2,1)S(1)} %convert_element_type.12.own_ref), custom_call_target="tpu_custom_call" | custom-call | tf_op jit(solution)/shard_map/pallas_call | solution.py:316
  63.7 0.0 copy-done.6
  63.7 0.6 dynamic_slice.3
  64.3 0.7 add_compare_fusion
  64.9 0.0 copy-done
  64.9 0.0 copy-done.5
  64.9 0.2 fusion.14
  65.1 1.9 %convolution_bitcast_fusion = f32[256,512]{1,0:T(8,128)S(1)} fusion(bf16[2048,512]{1,0:T(8,128)(2,1)S(1)} %bitcast.36, bf16[1,1,256,2048]{3,2,1,0:T(8,128)(2,1)} %param.9), kind=kOutput, calls=%fused_computation.5 | convolution fusion | flops 536870912 | bytes 3670016 | tf_op jit(solution)/shard_map/dot_general | solution.py:385
  67.1 0.1 fusion.11
  67.2 0.7 pad_maximum_fusion.own_ref
  67.9 0.0 copy-start.4
  67.9 0.0 copy-start.7
  67.9 0.0 copy-start.8
  67.9 40.7 %shard_map.121 = bf16[32,4,64,512]{3,2,1,0:T(8,128)(2,1)} custom-call(bf16[4,64,512]{2,1,0:T(8,128)(2,1)} %pad_maximum_fusion.own_ref), custom_call_target="tpu_custom_call" | custom-call | tf_op jit(solution)/shard_map/pallas_call | solution.py:235
  108.6 0.1 select_reduce_fusion
  108.8 0.0 all-to-all-done
  108.8 0.1 copy.15
  108.8 0.0 copy-done.4
  108.9 0.0 copy-done.7
  108.9 0.0 copy-done.8
  108.9 0.0 copy-start.2
  108.9 7.2 %fusion.19 = (bf16[4,64,512]{2,1,0:T(8,128)(2,1)S(1)}, f32[4,64,512]{2,1,0:T(8,128)}, f32[4,64,512]{2,1,0:T(8,128)}, f32[4,64,512]{2,1,0:T(8,128)}) fusion(f32[4,64,512]{2,1,0:T(8,128)S(1)} %copy-done.4, f32[4,64,512]{2,1,0:T(8,128)S(1)} %copy-done.7, f32[4,64,512]{2,1,0:T(8,128)S(1)} %copy-done.8, f32[4]{0:T(128)S(1)} %select_reduce_fusion, ...), kind=kOutput, calls=%fused_computation.30 | convolution fusion | flops 2151809024 | bytes 12877840 | tf_op jit(solution)/shard_map/dot_general | solution.py:400
  116.1 0.0 copy-done.2
  116.1 30.3 %shard_map.122 = bf16[32,64,512]{2,1,0:T(8,128)(2,1)S(1)} custom-call(s32[16]{0:T(128)S(1)} %copy-done.2, bf16[4,64,512]{2,1,0:T(8,128)(2,1)S(1)} %get-tuple-element.4.own_ref), custom_call_target="tpu_custom_call" | custom-call | tf_op jit(solution)/shard_map/pallas_call | solution.py:316
  146.5 1.3 copy.18
  (5 shorter events, 0.1 us)
Async XLA Ops:
  0.6 64.3 %copy-start = (bf16[1,1,256,256]{3,2,1,0:T(8,128)(2,1)S(1)}, bf16[1,1,256,256]{3,2,1,0:T(8,128)(2,1)}, u32[]{:S(2)}) copy-start(bf16[1,1,256,256]{3,2,1,0:T(8,128)(2,1)} %param.10) | copy-start | bytes 393220
  0.6 9.5 %copy-start.1 = (s32[16]{0:T(128)S(1)}, s32[16]{0:T(128)}, u32[]{:S(2)}) copy-start(s32[16]{0:T(128)} %slots_ref.2) | copy-start | bytes 196
  0.7 9.7 %copy-start.3 = (f32[4,64,512]{2,1,0:T(8,128)S(1)}, f32[4,64,512]{2,1,0:T(8,128)}, u32[]{:S(2)}) copy-start(f32[4,64,512]{2,1,0:T(8,128)} %param.15) | copy-start | bytes 1572868
  0.7 63.0 %copy-start.6 = (s32[2,16]{1,0:T(2,128)S(1)}, s32[2,16]{1,0:T(2,128)}, u32[]{:S(2)}) copy-start(s32[2,16]{1,0:T(2,128)} %param.12) | copy-start | bytes 388
  0.7 64.3 %copy-start.5 = (s32[1,1,4,64]{3,2,1,0:T(4,128)S(1)}, s32[1,1,4,64]{3,2,1,0:T(4,128)}, u32[]{:S(2)}) copy-start(s32[1,1,4,64]{3,2,1,0:T(4,128)} %param.11) | copy-start | bytes 3076
  3.0 105.8 %all-to-all-start = ((bf16[32,64,256]{2,1,0:T(8,128)(2,1)}), bf16[32,64,256]{2,1,0:T(8,128)(2,1)S(1)}, u32[]{:S(2)}, u32[]{:S(2)}) async-start(bf16[32,64,256]{2,1,0:T(8,128)(2,1)} %bitcast.2), calls=%async_computation | async-start | bytes 2097152 | tf_op jit(solution)/shard_map/all_to_all | solution.py:373
  67.9 40.9 %copy-start.4 = (f32[4,64,512]{2,1,0:T(8,128)S(1)}, f32[4,64,512]{2,1,0:T(8,128)}, u32[]{:S(2)}) copy-start(f32[4,64,512]{2,1,0:T(8,128)} %param.15) | copy-start | bytes 1572868
  67.9 40.9 %copy-start.7 = (f32[4,64,512]{2,1,0:T(8,128)S(1)}, f32[4,64,512]{2,1,0:T(8,128)}, u32[]{:S(2)}) copy-start(f32[4,64,512]{2,1,0:T(8,128)} %param.16) | copy-start | bytes 1572868
  67.9 40.9 %copy-start.8 = (f32[4,64,512]{2,1,0:T(8,128)S(1)}, f32[4,64,512]{2,1,0:T(8,128)}, u32[]{:S(2)}) copy-start(f32[4,64,512]{2,1,0:T(8,128)} %param.17) | copy-start | bytes 1572868
  108.9 7.3 %copy-start.2 = (s32[16]{0:T(128)S(1)}, s32[16]{0:T(128)}, u32[]{:S(2)}) copy-start(s32[16]{0:T(128)} %slots_ref.3) | copy-start | bytes 196

commit v4 on v3

--- a/solution.py
+++ b/solution.py
@@ -129,6 +129,51 @@
     pl.semaphore_wait(barrier, len(partners) + has_up + has_down)
 
 
+def shifts_of(levels):
+    steps = [(dy, dz, dx, dc) for dz in range(levels) for dy in (0, 1) for dx in (0, 1) for dc in (0, 1)]
+    return steps[1:]
+
+
+def meet_all(partners):
+    barrier = pltpu.get_barrier_semaphore()
+    for partner in partners:
+        pl.semaphore_signal(barrier, inc=1, device_id=partner, device_id_type=MESH)
+    pl.semaphore_wait(barrier, len(partners))
+
+
+def exchange(places, turned_ref, columns_ref, send_sem, recv_sem):
+    levels = places // 4
+    y, z, x, c = spot(places)
+    mine = y * places + z * 4 + x * 2 + c
+    steps = shifts_of(levels)
+    partners = [
+        device((y + dy) % 2, (z + dz) % levels, (x + dx) % 2, (c + dc) % 2)
+        for dy, dz, dx, dc in steps
+    ]
+
+    def copy(i, landing):
+        there = partners[i][0] * places + partners[i][1]
+        return remote(
+            turned_ref.at[there],
+            columns_ref.at[landing],
+            send_sem.at[i],
+            recv_sem.at[landing],
+            partners[i],
+        )
+
+    def start(dz):
+        for i, step in enumerate(steps):
+            if step[1] == dz:
+                copy(i, mine).start()
+
+    def end():
+        for i, partner in enumerate(partners):
+            copy(i, partner[0] * places + partner[1]).wait_recv()
+            copy(i, mine).wait_send()
+
+    return partners, mine, start, end
+
+
 def remote(source, target, send_sem, recv_sem, partner):
     return pltpu.make_async_remote_copy(
         src_ref=source,
@@ -140,7 +185,9 @@
     )
 
 
-def gather_kernel(places, own_ref, all_ref, send_sem, recv_sem, own_sem):
+def gather_kernel(
+    places, own_ref, turned_ref, all_ref, columns_ref, send_sem, recv_sem, own_sem, turn_send, turn_recv
+):
     levels = places // 4
     y, z, x, c = spot(places)
 
@@ -153,7 +200,8 @@
     first = device(y_first, z, x_first, c)
     last = device(y_last, z, x_last, c)
     sibling = device(y, z, x, 1 - c)
-    meet([first, last, sibling], z, levels, up, down)
+    everyone, mine, turn, turned = exchange(places, turned_ref, columns_ref, turn_send, turn_recv)
+    meet_all(everyone)
 
     def copy(kind, level, index, partner, source=None):
         return remote(
@@ -167,7 +215,6 @@
     def arrived(index):
         copy(0, 0, index, sibling).wait_recv()
 
-    mine = block(y, z, x, c)
     pl.when(z < levels - 1)(lambda: copy(0, z, mine, up, own_ref).start())
     pl.when(z > 0)(lambda: copy(1, z, mine, down, own_ref).start())
     copy(2, z, mine, first, own_ref).start()
@@ -175,6 +222,7 @@
     copy(4, z, mine, sibling, own_ref).start()
     keep = pltpu.make_async_copy(own_ref, all_ref.at[mine], own_sem)
     keep.start()
+    columns_ref[mine] = turned_ref[mine]
 
     def straight(level, below):
         index = block(y, level, x, c)
@@ -203,7 +251,9 @@
     for k in range(1, levels):
         both_ways(k, straight)
         both_ways(k - 1, over)
+        turn(k)
     both_ways(levels - 1, over)
+    turn(0)
 
     def ending(level, below):
         for kind, index in ((7, block(y_last, level, x_last, c)), (8, block(1 - y, level, 1 - x, c))):
@@ -217,6 +267,7 @@
             for group in range(2):
                 arrived(block(group, level, side, 1 - c))
     keep.wait()
+    turned()
     for level in range(levels):
         for kind in range(2, 9):
             copy(kind, level, mine, sibling).wait_send()
@@ -228,27 +279,37 @@
         )
 
 
-def whole_gather(shard):
+def whole_gather(shard, turned):
     places = lax.axis_size("place")
     devices = lax.axis_size("dp") * places
     levels = places // 4
     return pl.pallas_call(
         functools.partial(gather_kernel, places),
-        out_shape=jax.ShapeDtypeStruct((devices,) + shard.shape, shard.dtype),
-        in_specs=[pl.BlockSpec(memory_space=pl.ANY)],
-        out_specs=pl.BlockSpec(memory_space=pl.ANY),
+        out_shape=(
+            jax.ShapeDtypeStruct((devices,) + shard.shape, shard.dtype),
+            jax.ShapeDtypeStruct(turned.shape, turned.dtype),
+        ),
+        in_specs=[pl.BlockSpec(memory_space=pl.ANY), pl.BlockSpec(memory_space=pltpu.VMEM)],
+        out_specs=(pl.BlockSpec(memory_space=pl.ANY), pl.BlockSpec(memory_space=pltpu.VMEM)),
         scratch_shapes=[
             pltpu.SemaphoreType.DMA((9, levels)),
             pltpu.SemaphoreType.DMA((devices,)),
             pltpu.SemaphoreType.DMA,
+            pltpu.SemaphoreType.DMA((devices,)),
+            pltpu.SemaphoreType.DMA((devices,)),
         ],
-        compiler_params=pltpu.CompilerParams(collective_id=0, has_side_effects=True),
-    )(shard)
-
-
-def expert_kernel(
-    places, slots_ref, own_ref, out_ref, line, held, picked, line_send, line_recv, send_sem, recv_sem
-):
+        compiler_params=pltpu.CompilerParams(
+            collective_id=0, has_side_effects=True, vmem_limit_bytes=32 * 2**20
+        ),
+    )(shard, turned)
+
+
+def expert_kernel(places, turning, slots_ref, own_ref, *refs):
+    if turning:
+        turned_ref, out_ref, columns_ref, *refs = refs
+    else:
+        out_ref, *refs = refs
+    line, held, picked, line_send, line_recv, send_sem, recv_sem, *refs = refs
     levels = places // 4
     y, z, x, c = spot(places)
     up, down = device(y, z + 1, x, c), device(y, z - 1, x, c)
@@ -256,7 +317,11 @@
     plane = [((y + dy) % 2, (x + dx) % 2, (c + dc) % 2) for dy, dx, dc in shifts]
     partners = [device(there_y, z, there_x, there_c) for there_y, there_x, there_c in plane]
     line[z] = own_ref[...]
-    meet(partners, z, levels, up, down)
+    if turning:
+        everyone, mine, turn, turned = exchange(places, turned_ref, columns_ref, *refs)
+        meet_all(everyone)
+    else:
+        meet(partners, z, levels, up, down)
 
     def pass_on(way, level):
         return remote(
@@ -301,6 +366,12 @@
     for k in range(1, levels):
         pl.when(z >= k)(lambda k=k: below(z - k))
         pl.when(z < levels - k)(lambda k=k: above(z + k))
+        if turning:
+            turn(k)
+    if turning:
+        turn(0)
+        columns_ref[mine] = turned_ref[mine]
+        turned()
     for level in range(levels):
         for j, (there_y, there_x, there_c) in enumerate(plane):
             hand(j, level, there_y * places + level * 4 + there_x * 2 + there_c).wait()
@@ -308,19 +379,20 @@
         pl.when((z <= level) & (z > 0))(lambda level=level: pass_on(1, level).wait_send())
 
 
-def expert_rows(shard, slots):
+def expert_rows(shard, slots, turned=None):
     places = lax.axis_size("place")
     devices = lax.axis_size("dp") * places
     levels = places // 4
     tile = shard.shape[1:]
+    turning = turned is not None
+    extra = [turned] if turning else []
+    vmem = pl.BlockSpec(memory_space=pltpu.VMEM)
     return pl.pallas_call(
-        functools.partial(expert_kernel, places),
-        out_shape=jax.ShapeDtypeStruct((devices,) + tile, shard.dtype),
-        in_specs=[
-            pl.BlockSpec(memory_space=pltpu.SMEM),
-            pl.BlockSpec(memory_space=pltpu.VMEM),
-        ],
-        out_specs=pl.BlockSpec(memory_space=pltpu.VMEM),
+        functools.partial(expert_kernel, places, turning),
+        out_shape=[jax.ShapeDtypeStruct((devices,) + tile, shard.dtype)]
+        + [jax.ShapeDtypeStruct(array.shape, array.dtype) for array in extra],
+        in_specs=[pl.BlockSpec(memory_space=pltpu.SMEM), vmem] + [vmem for _ in extra],
+        out_specs=[vmem] + [vmem for _ in extra],
         scratch_shapes=[
             pltpu.VMEM((levels,) + shard.shape, shard.dtype),
             pltpu.VMEM(shard.shape, shard.dtype),
@@ -329,11 +401,12 @@
             pltpu.SemaphoreType.DMA((levels,)),
             pltpu.SemaphoreType.DMA((7, levels)),
             pltpu.SemaphoreType.DMA((devices,)),
-        ],
+        ]
+        + [pltpu.SemaphoreType.DMA((devices,)) for _ in range(2 * len(extra))],
         compiler_params=pltpu.CompilerParams(
-            collective_id=1, has_side_effects=True, vmem_limit_bytes=32 * 2**20
+            collective_id=1 + turning, has_side_effects=True, vmem_limit_bytes=32 * 2**20
         ),
-    )(slots, shard)
+    )(slots, shard, *extra)
 
 
 def adam(grad, master, first_moment, second_moment):
@@ -369,9 +442,9 @@
     rows, depth = rows_in.shape
     order = routing[0, 0]
     batches, batch_rows = order.shape
-    turned = rows_in.T.reshape(devices, rows_shard, rows)
-    columns = lax.all_to_all(turned, ("dp", "place"), split_axis=0, concat_axis=0, tiled=True)
-    weights = expert_rows(master.astype(jnp.bfloat16), old_slots).reshape(depth, width)
+    turned = rows_in.reshape(rows, devices, 2, rows_shard // 2).transpose(2, 1, 3, 0)
+    weights, upper = expert_rows(master.astype(jnp.bfloat16), old_slots, turned[0])
+    weights = weights.reshape(depth, width)
     live = jnp.arange(rows, dtype=jnp.int32) < row_count[group_here, place_here]
     place_of = (
         order[:, None, :] == jnp.arange(batch_rows, dtype=jnp.int32)[None, :, None]
@@ -391,11 +464,12 @@
     local = jnp.concatenate([incoming * upward * slope, incoming * active], axis=1).astype(
         jnp.bfloat16
     )
-    all_local = whole_gather(local.reshape(experts, rows * width // (experts * width), width))
+    all_local, lower = whole_gather(local, turned[1])
+    columns = jnp.concatenate([upper.transpose(1, 0, 2), lower.transpose(1, 0, 2)], axis=0)
     select = old_slots[None, :] == jnp.arange(experts, dtype=jnp.int32)[:, None]
     chosen = jnp.tile(select, (1, groups))
     stacked = jnp.where(
-        chosen[:, None, :, None], columns.transpose(1, 0, 2)[None], jnp.bfloat16(0)
+        chosen[:, None, :, None], columns[None], jnp.bfloat16(0)
     ).reshape(experts * rows_shard, devices * rows)
     grad_sum = jnp.dot(
         stacked, all_local.reshape(devices * rows, width), preferred_element_type=jnp.float32
@@ -404,7 +478,7 @@
     total = jnp.sum(jnp.where(select, per_slot[None, :], 0.0), axis=1)
     grad = grad_sum / total[:, None, None]
     new_master, new_first, new_second = adam(grad, master, first_moment, second_moment)
-    new_weights = expert_rows(new_master.astype(jnp.bfloat16), new_slots)
+    (new_weights,) = expert_rows(new_master.astype(jnp.bfloat16), new_slots)
     return (
         new_weights.reshape(1, depth, width),
         new_master,

time: 148 us -> 143 us (0.966)
  starting transfers between devices: 7.1 us -> 0 us
  Pallas kernels: 124 us -> 128 us
  matrix products: 9.36 us -> 5.4 us
  other arithmetic: 1.69 us -> 4.09 us
    all_to_all x1 -> x0, starting transfers between devices: 7.1 us -> none  [gathered(): lax.all_to_all(turned, ('dp', 'place'), split_axis=0, concat_axis=0, tile...]
    pallas_call x3, Pallas kernels: 124 us -> 128 us  [the longest x2 78.1 us: expert_rows(): pl.pallas_call(functools.partial(expert_kernel, places, turning), out_sha...]
    dot_general x1, matrix products: 7.24 us -> 3.86 us  [gathered(): jnp.dot(stacked, all_local.reshape(devices * rows, width), preferred_elem...]
    unnamed x22 -> x16, local copies, waits for them, and re-layouts: 3.82 us -> 3.32 us
  transfers between devices with their start and end apart: 1 -> 0, of which waited for: 0 -> 0; matrix products, arithmetic and copies ran while one was open for 3% -> 0% of each run, Pallas kernels for 64% -> 0%
where the time goes in v4:
time: 143 us
  Pallas kernels  128 us (90%)
  matrix products  5.4 us (4%)
  local copies, waits for them, and re-layouts  4.86 us (3%)
  other arithmetic  4.09 us (3%)
    pallas_call x2, Pallas kernels, expert_rows(): pl.pallas_call(functools.partial(expert_kernel, places, turning), out_sha...  78.1 us
    pallas_call x1, Pallas kernels, whole_gather(): pl.pallas_call(functools.partial(gather_kernel, places), out_shape=(jax.S...  49.6 us
    dot_general x1, matrix products, gathered(): jnp.dot(stacked, all_local.reshape(devices * rows, width), preferred_elem...  3.86 us
    unnamed x16, local copies, waits for them, and re-layouts  3.32 us

profile of v4, /device:TPU:1, one launch (start us, length us, event | category | flops | bytes accessed | tf_op | source)
XLA Modules:
  0.0 142.8 jit_solution(16703278764717124168)
XLA Ops:
  0.6 0.0 copy-start
  0.7 1.3 dynamic_slice.3
  2.0 0.7 add_compare_fusion
  2.6 0.0 copy-done
  2.6 0.7 convert_reduce_fusion
  3.3 0.8 select_reduce_fusion
  4.1 0.7 iota_compare_fusion.1
  4.8 0.1 tile.9
  4.8 0.8 fusion.22
  5.7 1.1 convert_element_type.11.own_ref
  6.8 1.5 %copy.14 = bf16[1,1,256,2048]{2,3,1,0:T(8,128)(2,1)S(1)} copy(bf16[1,1,256,2048]{3,2,1,0:T(8,128)(2,1)} %param.9) | data formatting | bytes 2097152 | tf_op args[0]
  8.3 0.0 copy-start.2
  8.3 0.0 copy-start.3
  8.3 0.1 copy.20
  8.4 0.1 slice_bitcast_fusion
  8.5 0.5 copy-done.2
  8.9 47.1 %shard_map.120 = (bf16[32,64,512]{2,1,0:T(8,128)(2,1)S(1)}, bf16[32,32,256]{2,1,0:T(8,128)(2,1)S(1)}) custom-call(s32[16]{0:T(128)S(1)} %copy-done.2, bf16[4,64,512]{2,1,0:T(8,128)(2,1)S(1)} %convert_element_type.11.own_ref, bf16[32,32,256]{2,1,0:T(8,128)(2,1)S(1)} %get-tuple-element.17.refs_0_), custom_call_target="tpu_custom_call" | custom-call | tf_op jit(solution)/shard_map/pallas_call | solution.py:390
  56.0 0.0 copy-done.3
  56.0 0.7 convolution_bitcast_fusion
  56.7 0.0 copy-start.4
  56.8 0.0 copy-start.5
  56.8 0.0 copy-start.6
  56.8 0.1 fusion.19
  56.9 49.6 %shard_map.121 = (bf16[32,256,512]{2,1,0:T(8,128)(2,1)S(1)}, bf16[32,32,256]{2,1,0:T(8,128)(2,1)S(1)}) custom-call(bf16[256,512]{1,0:T(8,128)(2,1)S(1)} %pad_maximum_fusion.1.own_ref, bf16[32,32,256]{2,1,0:T(8,128)(2,1)S(1)} %get-tuple-element.16.turned_ref), custom_call_target="tpu_custom_call" | custom-call | tf_op jit(solution)/shard_map/pallas_call | solution.py:286
  106.5 0.1 pad_maximum_fusion
  106.6 0.0 copy-done.4
  106.6 0.0 copy-done.5
  106.6 0.0 copy-done.6
  106.6 0.0 copy-start.1
  106.6 3.9 %fusion.27 = (bf16[4,64,512]{2,1,0:T(8,128)(2,1)S(1)}, f32[4,64,512]{2,1,0:T(8,128)}, f32[4,64,512]{2,1,0:T(8,128)}, f32[4,64,512]{2,1,0:T(8,128)}) fusion(f32[4,64,512]{2,1,0:T(8,128)S(1)} %copy-done.4, f32[4,64,512]{2,1,0:T(8,128)S(1)} %copy-done.5, f32[4,64,512]{2,1,0:T(8,128)S(1)} %copy-done.6, f32[4]{0:T(128)S(1)} %select_reduce_fusion, ...), kind=kOutput, calls=%fused_computation.35 | convolution fusion | flops 2151809024 | bytes 12845200 | tf_op jit(solution)/shard_map/dot_general | solution.py:474
  110.5 0.0 copy-done.1
  110.5 31.0 %shard_map.122 = bf16[32,64,512]{2,1,0:T(8,128)(2,1)S(1)} custom-call(s32[16]{0:T(128)S(1)} %copy-done.1, bf16[4,64,512]{2,1,0:T(8,128)(2,1)S(1)} %get-tuple-element.12.own_ref), custom_call_target="tpu_custom_call" | custom-call | tf_op jit(solution)/shard_map/pallas_call | solution.py:390
  141.5 1.3 copy.22
  (2 shorter events, 0.0 us)
Async XLA Ops:
  0.6 2.0 %copy-start = (bf16[1,1,256,256]{3,2,1,0:T(8,128)(2,1)S(1)}, bf16[1,1,256,256]{3,2,1,0:T(8,128)(2,1)}, u32[]{:S(2)}) copy-start(bf16[1,1,256,256]{3,2,1,0:T(8,128)(2,1)} %param.10) | copy-start | bytes 393220
  8.3 0.7 copy-start.2
  8.3 47.7 %copy-start.3 = (bf16[1,1,256,2048]{3,2,1,0:T(8,128)(2,1)S(1)}, bf16[1,1,256,2048]{3,2,1,0:T(8,128)(2,1)}, u32[]{:S(2)}) copy-start(bf16[1,1,256,2048]{3,2,1,0:T(8,128)(2,1)} %param.9) | copy-start | bytes 3145732
  56.7 49.9 %copy-start.4 = (f32[4,64,512]{2,1,0:T(8,128)S(1)}, f32[4,64,512]{2,1,0:T(8,128)}, u32[]{:S(2)}) copy-start(f32[4,64,512]{2,1,0:T(8,128)} %param.15) | copy-start | bytes 1572868
  56.8 49.9 %copy-start.5 = (f32[4,64,512]{2,1,0:T(8,128)S(1)}, f32[4,64,512]{2,1,0:T(8,128)}, u32[]{:S(2)}) copy-start(f32[4,64,512]{2,1,0:T(8,128)} %param.16) | copy-start | bytes 1572868
  56.8 49.9 %copy-start.6 = (f32[4,64,512]{2,1,0:T(8,128)S(1)}, f32[4,64,512]{2,1,0:T(8,128)}, u32[]{:S(2)}) copy-start(f32[4,64,512]{2,1,0:T(8,128)} %param.17) | copy-start | bytes 1572868
  106.6 3.9 %copy-start.1 = (s32[16]{0:T(128)S(1)}, s32[16]{0:T(128)}, u32[]{:S(2)}) copy-start(s32[16]{0:T(128)} %slots_ref.3) | copy-start | bytes 196

commit v5 on v4

--- a/solution.py
+++ b/solution.py
@@ -316,7 +316,7 @@
     shifts = [(0, 1, 0), (1, 0, 0), (0, 1, 1), (1, 0, 1), (1, 1, 0), (1, 1, 1), (0, 0, 1)]
     plane = [((y + dy) % 2, (x + dx) % 2, (c + dc) % 2) for dy, dx, dc in shifts]
     partners = [device(there_y, z, there_x, there_c) for there_y, there_x, there_c in plane]
-    line[z] = own_ref[...]
+    line[z] = own_ref[...].astype(line.dtype)
     if turning:
         everyone, mine, turn, turned = exchange(places, turned_ref, columns_ref, *refs)
         meet_all(everyone)
@@ -389,14 +389,14 @@
     vmem = pl.BlockSpec(memory_space=pltpu.VMEM)
     return pl.pallas_call(
         functools.partial(expert_kernel, places, turning),
-        out_shape=[jax.ShapeDtypeStruct((devices,) + tile, shard.dtype)]
+        out_shape=[jax.ShapeDtypeStruct((devices,) + tile, jnp.bfloat16)]
         + [jax.ShapeDtypeStruct(array.shape, array.dtype) for array in extra],
         in_specs=[pl.BlockSpec(memory_space=pltpu.SMEM), vmem] + [vmem for _ in extra],
         out_specs=[vmem] + [vmem for _ in extra],
         scratch_shapes=[
-            pltpu.VMEM((levels,) + shard.shape, shard.dtype),
-            pltpu.VMEM(shard.shape, shard.dtype),
-            pltpu.VMEM((7, levels) + tile, shard.dtype),
+            pltpu.VMEM((levels,) + shard.shape, jnp.bfloat16),
+            pltpu.VMEM(shard.shape, jnp.bfloat16),
+            pltpu.VMEM((7, levels) + tile, jnp.bfloat16),
             pltpu.SemaphoreType.DMA((2, levels)),
             pltpu.SemaphoreType.DMA((levels,)),
             pltpu.SemaphoreType.DMA((7, levels)),
@@ -443,7 +443,7 @@
     order = routing[0, 0]
     batches, batch_rows = order.shape
     turned = rows_in.reshape(rows, devices, 2, rows_shard // 2).transpose(2, 1, 3, 0)
-    weights, upper = expert_rows(master.astype(jnp.bfloat16), old_slots, turned[0])
+    weights, upper = expert_rows(master, old_slots, turned[0])
     weights = weights.reshape(depth, width)
     live = jnp.arange(rows, dtype=jnp.int32) < row_count[group_here, place_here]
     place_of = (
@@ -474,11 +474,11 @@
     grad_sum = jnp.dot(
         stacked, all_local.reshape(devices * rows, width), preferred_element_type=jnp.float32
     ).reshape(experts, rows_shard, width)
-    per_slot = jnp.sum(row_count.astype(jnp.float32), axis=0)
-    total = jnp.sum(jnp.where(select, per_slot[None, :], 0.0), axis=1)
+    counts = row_count.astype(jnp.float32)
+    total = jnp.sum(jnp.where(select[:, None, :], counts[None], 0.0), axis=(1, 2))
     grad = grad_sum / total[:, None, None]
     new_master, new_first, new_second = adam(grad, master, first_moment, second_moment)
-    (new_weights,) = expert_rows(new_master.astype(jnp.bfloat16), new_slots)
+    (new_weights,) = expert_rows(new_master, new_slots)
     return (
         new_weights.reshape(1, depth, width),
         new_master,

time: 143 us -> 141 us (0.986)
  other arithmetic: 4.09 us -> 2.35 us
    unnamed x16 -> x18, local copies, waits for them, and re-layouts: 3.32 us -> 3.7 us
where the time goes in v5:
time: 141 us
  Pallas kernels  128 us (91%)
  local copies, waits for them, and re-layouts  5.24 us (4%)
  matrix products  5.22 us (4%)
  other arithmetic  2.35 us (2%)
    pallas_call x2, Pallas kernels, expert_rows(): pl.pallas_call(functools.partial(expert_kernel, places, turning), out_sha...  78.1 us
    pallas_call x1, Pallas kernels, whole_gather(): pl.pallas_call(functools.partial(gather_kernel, places), out_shape=(jax.S...  49.6 us
    unnamed x18, local copies, waits for them, and re-layouts  3.7 us
    dot_general x1, matrix products, gathered(): jnp.dot(stacked, all_local.reshape(devices * rows, width), preferred_elem...  3.68 us

profile of v5, /device:TPU:1, one launch (start us, length us, event | category | flops | bytes accessed | tf_op | source)
XLA Modules:
  0.0 141.2 jit_solution(2667238956920913083)
XLA Ops:
  0.6 0.0 copy-start
  0.7 1.3 dynamic_slice.3
  2.0 0.7 add_compare_fusion
  2.6 0.0 copy-done
  2.6 0.7 iota_compare_fusion.1
  3.3 0.7 convert_element_type.2
  4.0 0.1 select_reduce_fusion
  4.1 0.1 tile.9
  4.2 0.8 fusion.22
  5.0 1.5 %copy.14 = bf16[1,1,256,2048]{2,3,1,0:T(8,128)(2,1)S(1)} copy(bf16[1,1,256,2048]{3,2,1,0:T(8,128)(2,1)} %param.9) | data formatting | bytes 2097152 | tf_op args[0]
  6.5 0.0 copy-start.1
  6.5 0.0 copy-start.3
  6.5 0.1 copy.20
  6.6 0.0 copy-start.5
  6.6 0.1 slice_bitcast_fusion
  6.7 0.8 copy-done.1
  7.6 0.0 copy-done.3
  7.6 47.1 %shard_map.120 = (bf16[32,64,512]{2,1,0:T(8,128)(2,1)S(1)}, bf16[32,32,256]{2,1,0:T(8,128)(2,1)S(1)}) custom-call(s32[16]{0:T(128)S(1)} %copy-done.3, f32[4,64,512]{2,1,0:T(8,128)S(1)} %copy-done.1, bf16[32,32,256]{2,1,0:T(8,128)(2,1)S(1)} %get-tuple-element.16.refs_0_), custom_call_target="tpu_custom_call" | custom-call | tf_op jit(solution)/shard_map/pallas_call | solution.py:390
  54.7 0.0 copy-done.5
  54.7 0.7 convolution_bitcast_fusion
  55.4 0.0 copy-start.6
  55.4 0.0 copy-start.7
  55.4 0.1 fusion.19
  55.6 49.6 %shard_map.121 = (bf16[32,256,512]{2,1,0:T(8,128)(2,1)S(1)}, bf16[32,32,256]{2,1,0:T(8,128)(2,1)S(1)}) custom-call(bf16[256,512]{1,0:T(8,128)(2,1)S(1)} %pad_maximum_fusion.1.own_ref, bf16[32,32,256]{2,1,0:T(8,128)(2,1)S(1)} %get-tuple-element.15.turned_ref), custom_call_target="tpu_custom_call" | custom-call | tf_op jit(solution)/shard_map/pallas_call | solution.py:286
  105.1 0.1 pad_maximum_fusion
  105.2 0.0 copy-done.6
  105.2 0.0 copy-done.7
  105.2 0.0 copy-start.4
  105.3 3.7 %multiply_subtract_fusion = (f32[4,64,512]{2,1,0:T(8,128)S(1)}, f32[4,64,512]{2,1,0:T(8,128)}, f32[4,64,512]{2,1,0:T(8,128)}) fusion(f32[4,64,512]{2,1,0:T(8,128)S(1)} %copy-done.1, f32[4,64,512]{2,1,0:T(8,128)S(1)} %copy-done.6, f32[4,64,512]{2,1,0:T(8,128)S(1)} %copy-done.7, f32[4]{0:T(128)S(1)} %select_reduce_fusion, ...), kind=kOutput, calls=%fused_computation.16 | convolution fusion | flops 2151677952 | bytes 12583056 | tf_op jit(solution)/shard_map/dot_general | solution.py:474
  108.9 0.0 copy-start.2
  108.9 0.0 copy-done.4
  108.9 31.0 %shard_map.122 = bf16[32,64,512]{2,1,0:T(8,128)(2,1)S(1)} custom-call(s32[16]{0:T(128)S(1)} %copy-done.4, f32[4,64,512]{2,1,0:T(8,128)S(1)} %get-tuple-element.24.own_ref), custom_call_target="tpu_custom_call" | custom-call | tf_op jit(solution)/shard_map/pallas_call | solution.py:390
  139.9 1.3 copy.22
  141.2 0.0 copy-done.2
  (2 shorter events, 0.0 us)
Async XLA Ops:
  0.6 2.0 %copy-start = (bf16[1,1,256,256]{3,2,1,0:T(8,128)(2,1)S(1)}, bf16[1,1,256,256]{3,2,1,0:T(8,128)(2,1)}, u32[]{:S(2)}) copy-start(bf16[1,1,256,256]{3,2,1,0:T(8,128)(2,1)} %param.10) | copy-start | bytes 393220
  6.5 1.0 copy-start.1
  6.5 1.0 copy-start.3
  6.6 48.0 %copy-start.5 = (bf16[1,1,256,2048]{3,2,1,0:T(8,128)(2,1)S(1)}, bf16[1,1,256,2048]{3,2,1,0:T(8,128)(2,1)}, u32[]{:S(2)}) copy-start(bf16[1,1,256,2048]{3,2,1,0:T(8,128)(2,1)} %param.9) | copy-start | bytes 3145732
  55.4 49.8 %copy-start.6 = (f32[4,64,512]{2,1,0:T(8,128)S(1)}, f32[4,64,512]{2,1,0:T(8,128)}, u32[]{:S(2)}) copy-start(f32[4,64,512]{2,1,0:T(8,128)} %param.16) | copy-start | bytes 1572868
  55.4 49.8 %copy-start.7 = (f32[4,64,512]{2,1,0:T(8,128)S(1)}, f32[4,64,512]{2,1,0:T(8,128)}, u32[]{:S(2)}) copy-start(f32[4,64,512]{2,1,0:T(8,128)} %param.17) | copy-start | bytes 1572868
  105.2 3.7 %copy-start.4 = (s32[16]{0:T(128)S(1)}, s32[16]{0:T(128)}, u32[]{:S(2)}) copy-start(s32[16]{0:T(128)} %slots_ref.3) | copy-start | bytes 196
  108.9 32.3 %copy-start.2 = (f32[4,64,512]{2,1,0:T(8,128)}, f32[4,64,512]{2,1,0:T(8,128)S(1)}, u32[]{:S(2)}) copy-start(f32[4,64,512]{2,1,0:T(8,128)S(1)} %get-tuple-element.24.own_ref) | copy-start | bytes 1572868
